TPU v7x, 32 devices: a whole 2x2x4 slice. The times are simulated.
32 devices in a mesh: req: 2 (over x), head: 4 (over y, core), row: 4 (over z).
Axes of the slice: x: 2, y: 2, z: 4, core: 2. Of those that a mesh axis runs over, the one named last changes fastest.
Arguments:
- incoming_activations: bfloat16 [32, 4, 2048], P(('req', 'head'), None, 'row'), may hold values from -6 to 6
- genuine_symbol_number: int32 [32], replicated, may hold values from 1 to 4, as said below
- caller_sheet_slot: int32 [32], replicated, may hold values from 0 to 31, as said below
- memory_sheets: float32 [32, 32, 4096], P('req', 'head', 'row'), may hold values from -4 to 4
- prior_activation_sheets: float32 [32, 2048], P('req', 'row'), may hold values from -6 to 6
- blend_fractions: float32 [5, 2048], P(None, 'row'), may hold values from 0 to 1
- first_projectors: bfloat16 [3, 2048, 2048], P(None, 'row', 'head'), may hold values from -0.125 to 0.125
- fading_narrow_projector: bfloat16 [2048, 96], P('row'), may hold values from -0.125 to 0.125
- fading_widen_projector: bfloat16 [96, 2048], P(None, 'head'), may hold values from -0.625 to 0.625
- fading_offset: float32 [2048], P('head'), may hold values from -5 to 1
- context_step_narrowing: bfloat16 [2048, 96], P('row'), may hold values from -0.125 to 0.125
- context_step_widening: bfloat16 [96, 2048], P(None, 'head'), may hold values from -0.625 to 0.625
- context_step_offset: float32 [2048], P('head'), may hold values from -2 to 2
- erasure_address_gain: float32 [2048], P('head'), may hold values from 0.25 to 2
- address_correction: float32 [2048], P('head'), may hold values from 0 to 1.5
- reward_coefficients: float32 [32, 64], P('head'), may hold values from -0.6 to 0.6
- groupwise_gain: float32 [32, 64], P('head', 'row'), may hold values from 0.5 to 1.5
- final_projector: bfloat16 [32, 64, 2048], P('head', 'row'), may hold values from -0.125 to 0.125
Outputs:
- mixed: bfloat16 [32, 4, 2048], P(('req', 'head'), None, 'row')
- new_state: float32 [32, 32, 4096], P('req', 'head', 'row')
- new_shift: float32 [32, 2048], P('req', 'row')
Inputs may be any that keep to these rules, and one draw needn't show every extreme that they name: `genuine_symbol_number`: every request has 1 or 4 valid tokens; the share with 4 differs between indices of req. `caller_sheet_slot`: a permutation; the pages of index i of req are i * 16 to (i + 1) * 16 - 1; for any two indices of req, between 7 and 8 of the first one's requests have their pages on the second.
All inputs are finite; a program needn't handle non-finite values.
Results may differ from a plain program's by a relative error of at most 0.02.
Values may be sent and summed in bfloat16 or wider, within the bound.
A program may use at most 64 MiB of HBM per device.

v0:
```python
import jax
import jax.numpy as jnp
from jax import lax
from jax.sharding import PartitionSpec as P

CHANNEL_SPAN = 64
TS = 4
REQ_DEV = 16


def project(token_rows, weight):
    return jnp.einsum("rtd,de->rte", token_rows, weight, preferred_element_type=jnp.float32)


def invert_slots(slots, total_slots):
    width_now = slots.shape[0]
    matches = slots[None, :] == jnp.arange(total_slots, dtype=jnp.int32)[:, None]
    anchor = jnp.sum(jnp.where(matches, jnp.arange(width_now, dtype=jnp.int32)[None, :], 0), axis=1)
    return anchor + jnp.where(jnp.any(matches, axis=1), 0, width_now)


def pick_rows(values, positions):
    padded = jnp.concatenate([values, jnp.zeros_like(values[:1])], axis=0)
    return jnp.take(padded, positions, axis=0)


def slot_tables(genuine_symbol_number, caller_sheet_slot, device, groups, capacity):
    owners = caller_sheet_slot // REQ_DEV
    blocks = owners.reshape(groups, REQ_DEV)
    same_owner = (blocks[:, :, None] == blocks[:, None, :]).astype(jnp.int32)
    positions = jnp.arange(REQ_DEV, dtype=jnp.int32)
    earlier = (positions[None, :] < positions[:, None]).astype(jnp.int32)
    rank_all = jnp.sum(same_owner * earlier[None], axis=2).reshape(-1)
    start_row = device * REQ_DEV
    my_owner = lax.dynamic_slice_in_dim(owners, start_row, REQ_DEV)
    my_rank = lax.dynamic_slice_in_dim(rank_all, start_row, REQ_DEV)
    request_slots = my_owner * capacity + my_rank
    request_valid = lax.dynamic_slice_in_dim(genuine_symbol_number, start_row, REQ_DEV)
    all_requests = jnp.arange(caller_sheet_slot.shape[0], dtype=jnp.int32)
    holder = caller_sheet_slot[None, :] == (start_row + positions)[:, None]
    requester = jnp.sum(jnp.where(holder, all_requests[None, :], 0), axis=1)
    page_slots = requester // REQ_DEV * capacity + jnp.take(rank_all, requester)
    page_valid = jnp.take(genuine_symbol_number, requester)
    return (request_slots, request_valid, page_slots, page_valid)


def time_mix(
    token_rows,
    live_count,
    state_now,
    shift_row,
    blend_fractions,
    first_projectors,
    fading_narrow_projector,
    fading_widen_projector,
    fading_offset,
    context_step_narrowing,
    context_step_widening,
    context_step_offset,
    erasure_address_gain,
    address_correction,
    reward_coefficients,
    groupwise_gain,
):
    requests = token_rows.shape[0]
    local_heads = groupwise_gain.shape[0]
    value_rows = groupwise_gain.shape[1]
    row_count = lax.axis_size("row")
    current = token_rows.astype(jnp.float32)
    before = jnp.concatenate([shift_row[:, None, :], current[:, :-1, :]], axis=1)
    towards = before - current
    mixed_in = [
        (current + towards * blend_fractions[branch]).astype(jnp.bfloat16) for branch in range(5)
    ]
    recept_part = project(mixed_in[0], first_projectors[0])
    key_part = project(mixed_in[2], first_projectors[1])
    value_part = project(mixed_in[3], first_projectors[2])
    decay_part = project(mixed_in[1], fading_narrow_projector)
    learn_part = project(mixed_in[4], context_step_narrowing)
    acceptance_query, key_vec, decay_sum, learn_sum = lax.psum(
        (recept_part, key_part, decay_part, learn_part), "row"
    )
    split_values = value_part.reshape(requests, TS, local_heads, row_count, value_rows)
    payload_entries = lax.psum_scatter(
        split_values, "row", scatter_dimension=3, tiled=True
    ).reshape(requests, TS, local_heads, value_rows)
    heads_shape = (requests, TS, local_heads, CHANNEL_SPAN)
    decay_low = jnp.tanh(decay_sum).astype(jnp.bfloat16)
    log_rate = -jax.nn.softplus(-(fading_offset + project(decay_low, fading_widen_projector))) - 0.5
    decay_rate = jnp.exp(-jnp.exp(log_rate)).reshape(heads_shape)
    learn_flat = jax.nn.sigmoid(
        context_step_offset + project(learn_sum.astype(jnp.bfloat16), context_step_widening)
    )
    learn_rate = learn_flat.reshape(heads_shape)
    scaled = (key_vec * erasure_address_gain).reshape(heads_shape)
    key_dir = scaled / jnp.sqrt(jnp.sum(scaled * scaled, axis=-1, keepdims=True) + 1e-06)
    address_corrected = (key_vec * (1.0 + (learn_flat - 1.0) * address_correction)).reshape(
        heads_shape
    )
    acceptance_query = acceptance_query.reshape(heads_shape)
    outputs = []
    for position in range(TS):
        live_now = (position < live_count)[:, None, None, None]
        removed = jnp.sum(state_now * (-key_dir[:, position])[:, :, None, :], axis=-1)
        update = state_now * decay_rate[:, position][:, :, None, :]
        update = (
            update
            + removed[..., None] * (key_dir[:, position] * learn_rate[:, position])[:, :, None, :]
        )
        update = (
            update
            + payload_entries[:, position][..., None]
            * address_corrected[:, position][:, :, None, :]
        )
        state_now = jnp.where(live_now, update, state_now)
        reading = jnp.sum(state_now * acceptance_query[:, position][:, :, None, :], axis=-1)
        outputs.append(jnp.where(live_now[..., 0], reading, jnp.zeros_like(reading)))
    groupwise_results = jnp.stack(outputs, axis=1)
    genuine_symbol_filter = (jnp.arange(TS)[None, :] < live_count[:, None])[:, :, None, None]
    reward_multiplier = jnp.sum(
        acceptance_query * address_corrected * reward_coefficients, axis=-1, keepdims=True
    )
    reward_summand = jnp.where(
        genuine_symbol_filter, reward_multiplier * payload_entries, jnp.zeros_like(payload_entries)
    )
    head_sum = lax.psum(jnp.sum(groupwise_results, axis=-1), "row")
    demeaned_entries = head_sum / CHANNEL_SPAN
    offset = groupwise_results - demeaned_entries[..., None]
    groupwise_spread = lax.psum(jnp.sum(offset * offset, axis=-1), "row") / CHANNEL_SPAN
    standardised_groups = (
        (groupwise_results - demeaned_entries[..., None])
        / jnp.sqrt(groupwise_spread[..., None] + 0.00064)
        * groupwise_gain
        + reward_summand
    ).astype(jnp.bfloat16)
    last_token = jnp.take_along_axis(current, (live_count - 1)[:, None, None], axis=1)[:, 0]
    return (state_now, last_token, standardised_groups)


def per_device(
    incoming_activations,
    genuine_symbol_number,
    caller_sheet_slot,
    memory_sheets,
    prior_activation_sheets,
    blend_fractions,
    first_projectors,
    fading_narrow_projector,
    fading_widen_projector,
    fading_offset,
    context_step_narrowing,
    context_step_widening,
    context_step_offset,
    erasure_address_gain,
    address_correction,
    reward_coefficients,
    groupwise_gain,
    final_projector,
):
    req_count = lax.axis_size("req")
    head_count = lax.axis_size("head")
    row_count = lax.axis_size("row")
    capacity = (REQ_DEV + req_count - 1) // req_count
    slot_count = req_count * capacity
    device = lax.axis_index("req")
    request_slots, request_valid, page_slots, page_valid = slot_tables(
        genuine_symbol_number, caller_sheet_slot, device, req_count, capacity
    )
    gathered = lax.all_gather(incoming_activations, "head", axis=0, tiled=True)
    local_heads = memory_sheets.shape[1]
    value_rows = groupwise_gain.shape[1]
    leaving = invert_slots(page_slots, slot_count)
    state_got, shift_got = (
        lax.all_to_all(
            pick_rows(memory_sheets, leaving), "req", split_axis=0, concat_axis=0, tiled=True
        ),
        lax.all_to_all(
            pick_rows(prior_activation_sheets, leaving),
            "req",
            split_axis=0,
            concat_axis=0,
            tiled=True,
        ),
    )
    state_now = jnp.take(state_got, request_slots, axis=0).reshape(
        REQ_DEV, local_heads, value_rows, CHANNEL_SPAN
    )
    shift_now = jnp.take(shift_got, request_slots, axis=0)
    state_new, last_token, standardised_groups = time_mix(
        gathered,
        request_valid,
        state_now,
        shift_now,
        blend_fractions,
        first_projectors,
        fading_narrow_projector,
        fading_widen_projector,
        fading_offset,
        context_step_narrowing,
        context_step_widening,
        context_step_offset,
        erasure_address_gain,
        address_correction,
        reward_coefficients,
        groupwise_gain,
    )
    homeward = invert_slots(request_slots, slot_count)
    flat_state = state_new.reshape(REQ_DEV, local_heads, value_rows * CHANNEL_SPAN)
    state_back, shift_back = (
        lax.all_to_all(
            pick_rows(flat_state, homeward).astype(jnp.bfloat16),
            "req",
            split_axis=0,
            concat_axis=0,
            tiled=True,
        ).astype(jnp.float32),
        lax.all_to_all(
            pick_rows(last_token, homeward).astype(jnp.bfloat16),
            "req",
            split_axis=0,
            concat_axis=0,
            tiled=True,
        ).astype(jnp.float32),
    )
    new_state = jnp.take(state_back, page_slots, axis=0)
    new_shift = jnp.take(shift_back, page_slots, axis=0)
    grouped = standardised_groups.reshape(
        head_count, REQ_DEV // head_count, TS, local_heads * value_rows
    )
    columns = final_projector.reshape(
        local_heads * value_rows, row_count, final_projector.shape[2] // row_count
    )
    terms = jnp.einsum("hqtf,fcd->hcqtd", grouped, columns, preferred_element_type=jnp.float32)
    terms = terms.reshape(head_count * row_count * (REQ_DEV // head_count), TS, columns.shape[2])
    mixed = lax.psum_scatter(
        terms.astype(jnp.bfloat16), ("head", "row"), scatter_dimension=0, tiled=True
    )
    return (mixed, new_state, new_shift)


def solution(mesh):
    placed = (
        P(("req", "head"), None, "row"),
        P(),
        P(),
        P("req", "head", "row"),
        P("req", "row"),
        P(None, "row"),
        P(None, "row", "head"),
        P("row", None),
        P(None, "head"),
        P("head"),
        P("row", None),
        P(None, "head"),
        P("head"),
        P("head"),
        P("head"),
        P("head", None),
        P("head", "row"),
        P("head", "row", None),
    )
    return jax.shard_map(
        per_device,
        mesh=mesh,
        in_specs=placed,
        out_specs=(P(("req", "head"), None, "row"), P("req", "head", "row"), P("req", "row")),
        check_vma=False,
    )
```

profile of v0, /device:TPU:0, one launch (start us, length us, event | category | flops | bytes accessed | tf_op | source)
XLA Modules:
  0.0 327.0 jit_solution(17321454910995530649)
XLA Ops:
  9.5 6.5 %all_gather.3 = bf16[16,4,512]{2,1,0:T(4,128)(2,1)S(1)} all-gather(bf16[4,4,512]{2,1,0:T(4,128)(2,1)} %param.26), channel_id=1, replica_groups=mesh['req'=2,'head'=4,'row'=4] {'head'}, dimensions={0}, use_global_device_ids=true | all-gather | bytes 81920 | tf_op jit(solution)/shard_map/all_gather | solution.py:169
  18.0 3.2 all-to-all-start.3
  21.8 0.8 select_reduce_fusion.3
  23.6 0.9 fusion.82
  24.5 1.1 slice_bitcast_fusion
  27.6 0.9 broadcast_select_fusion.2
  31.0 3.3 %all-to-all-start.1 = ((f32[2,8,512]{2,1,0:T(8,128)}), f32[2,8,512]{2,1,0:T(8,128)S(1)}, u32[]{:S(2)}, u32[]{:S(2)}) async-start(f32[2,8,512]{2,1,0:T(8,128)} %select_bitcast_fusion.1), calls=%async_computation.1 | async-start | bytes 65536 | tf_op jit(solution)/shard_map/all_to_all | solution.py:177
  35.6 2.7 all-to-all-done.1
  38.2 3.5 %all-to-all-start = ((f32[16,8,1024]{2,1,0:T(8,128)}), f32[16,8,1024]{2,1,0:T(8,128)S(1)}, u32[]{:S(2)}, u32[]{:S(2)}) async-start(f32[16,8,1024]{2,1,0:T(8,128)} %broadcast_select_fusion.2), calls=%async_computation | async-start | bytes 1048576 | tf_op jit(solution)/shard_map/all_to_all | solution.py:174
  42.4 1.9 fusion.21
  44.4 1.3 fusion.19
  46.0 20.6 %all-reduce.6 = (bf16[16,4,96]{2,0,1:T(8,128)(2,1)S(1)}, f32[16,4,96]{2,0,1:T(8,128)S(1)}) all-reduce(f32[16,4,96]{2,0,1:T(8,128)S(1)} %fusion.40, f32[16,4,96]{2,0,1:T(8,128)S(1)} %fusion.43), channel_id=1, replica_groups=mesh['req'=2,'head'=4,'row'=4] {'row'}, use_global_device_ids=true, to_apply=%region_8.13 | all-reduce | flops 12288 | bytes 86016 | tf_op jit(solution)/shard_map/psum | solution.py:80
  66.5 1.9 fusion.47
  68.7 0.8 reshape.446
  69.8 1.1 mul.581
  71.0 1.1 mul.577
  72.2 1.1 mul.573
  73.4 1.1 mul.569
  75.5 58.6 %all-reduce.13.cloned.1.call-done = (f32[16,4,8,64]{3,2,0,1:T(8,128)}, f32[16,4,512]{2,0,1:T(8,128)}, f32[16,4,8,4,16]{4,0,3,2,1:T(8,128)}) async-done(((f32[16,4,8,64]{3,2,0,1:T(8,128)}, f32[16,4,512]{2,0,1:T(8,128)}, f32[16,4,8,4,16]{4,0,3,2,1:T(8,128)}), (f32[16,4,8,64]{3,2,0,1:T(8,128)}, f32[16,4,512]{2,0,1:T(8,128)}, f32[16,4,8,4,16]{4,0,3,2,1:T(8,128)})) %all-reduce.13.cloned.1.call-update) | async-done | bytes 393232 | tf_op jit(solution)/shard_map/psum | solution.py:80
  134.2 1.8 broadcast_multiply_fusion.4
  138.7 1.6 constant_dynamic-slice_fusion.1
  141.1 1.0 reshape.443
  142.9 5.0 %multiply_reduce_fusion.3 = (f32[16,8,16]{2,1,0:T(8,128)}, f32[16,8,16,64]{3,2,1,0:T(8,128)S(1)}, f32[16,8,16,64]{3,2,1,0:T(8,128)}, f32[16,8,16,64]{3,2,1,0:T(8,128)}) fusion(f32[16,8,64]{2,1,0:T(8,128)} %get-tuple-element.51, f32[16,8,16,64]{3,2,1,0:T(8,128)S(1)} %reshape.440, f32[16,8,64]{2,1,0:T(8,128)} %get-tuple-element.47, ...), kind=kOutput, calls=%fused_computation.32 | output fusion | flops 1179711 | bytes 2277392 | tf_op jit(solution)/shard_map/mul | solution.py:108
  147.9 2.4 mul.572
  150.4 1.1 mul.571
  151.5 5.1 %multiply_reduce_fusion.2 = (f32[16,8,16]{2,1,0:T(8,128)}, f32[16,8,16,64]{3,2,1,0:T(8,128)S(1)}, f32[16,8,16,64]{3,2,1,0:T(8,128)}, f32[16,8,16,64]{3,2,1,0:T(8,128)}) fusion(f32[16,8,64]{2,1,0:T(8,128)} %get-tuple-element.50, f32[16,8,16,64]{3,2,1,0:T(8,128)S(1)} %get-tuple-element.21, f32[16,8,64]{2,1,0:T(8,128)} %get-tuple-element.46, ...), kind=kOutput, calls=%fused_computation.30 | output fusion | flops 1179711 | bytes 2277392 | tf_op jit(solution)/shard_map/mul | solution.py:108
  156.6 2.4 mul.576
  159.0 1.1 mul.575
  160.1 4.5 %broadcast_multiply_fusion.1 = (f32[16,8,16,64]{3,2,1,0:T(8,128)}, f32[16,8,16,64]{3,2,1,0:T(8,128)}, f32[16,8,16,64]{3,2,1,0:T(8,128)S(1)}) fusion(f32[16,8,64]{2,1,0:T(8,128)} %get-tuple-element.45, f32[16,8,16]{2,1,0:T(8,128)} %get-tuple-element.41, f32[16,8,16,64]{3,2,1,0:T(8,128)S(1)} %get-tuple-element.23, f32[16,8,64]{2,1,0:T(8,128)} %copy-done.13, ...), kind=kOutput, calls=%fused_computation.51 | output fusion | flops 919615 | bytes 2236432 | tf_op jit(solution)/shard_map/mul | solution.py:108
  164.6 2.4 mul.580
  167.0 1.1 mul.579
  168.1 1.0 bitcast_select_fusion.2
  169.1 4.4 %multiply_reduce_fusion.1 = (f32[16,8,16]{2,1,0:T(8,128)S(1)}, f32[16,8,16]{2,1,0:T(8,128)S(1)}, f32[16,8,16,64]{3,2,1,0:T(8,128)}, f32[16,8,16,64]{3,2,1,0:T(8,128)S(1)}) fusion(f32[16,8,16,64]{3,2,1,0:T(8,128)S(1)} %copy-done.3, f32[16,8,64]{2,1,0:T(8,128)} %get-tuple-element.49, f32[16,8,64]{2,1,0:T(8,128)} %get-tuple-element.48, ...), kind=kOutput, calls=%fused_computation.28 | output fusion | flops 1439807 | bytes 1794064 | tf_op jit(solution)/shard_map/mul | solution.py:108
  174.4 17.7 %psum.46 = f32[16,4,8]{2,0,1:T(8,128)} all-reduce(f32[16,4,8]{2,0,1:T(8,128)S(1)} %fusion.61), channel_id=1, replica_groups=mesh['req'=2,'head'=4,'row'=4] {'row'}, use_global_device_ids=true, to_apply=%region_19.24 | all-reduce | flops 512 | bytes 4096 | tf_op jit(solution)/shard_map/psum | solution.py:126
  192.8 1.8 multiply_reduce_fusion.9
  194.7 17.4 %psum.47 = f32[16,4,8]{2,0,1:T(8,128)} all-reduce(f32[16,4,8]{2,0,1:T(8,128)} %multiply_reduce_fusion.9), channel_id=1, replica_groups=mesh['req'=2,'head'=4,'row'=4] {'row'}, use_global_device_ids=true, to_apply=%region_21.26 | all-reduce | flops 512 | bytes 4096 | tf_op jit(solution)/shard_map/psum | solution.py:129
  212.9 2.0 add_convert_fusion
  214.8 1.0 reshape.564
  215.9 1.1 mul.584
  217.0 1.1 mul.583
  218.2 2.9 add_select_fusion.3
  221.9 0.8 select_convert_fusion
  222.7 3.4 %all-to-all-start.2 = ((bf16[16,8,1024]{2,1,0:T(8,128)(2,1)}), bf16[16,8,1024]{2,1,0:T(8,128)(2,1)S(1)}, u32[]{:S(2)}, u32[]{:S(2)}) async-start(bf16[16,8,1024]{2,1,0:T(8,128)(2,1)} %select_convert_fusion), calls=%async_computation.2 | async-start | bytes 524288 | tf_op jit(solution)/shard_map/all_to_all | solution.py:210
  226.5 0.8 copy.70
  227.4 4.0 %all-to-all-done.2 = bf16[16,8,1024]{2,1,0:T(8,128)(2,1)S(1)} async-done(((bf16[16,8,1024]{2,1,0:T(8,128)(2,1)}), bf16[16,8,1024]{2,1,0:T(8,128)(2,1)S(1)}, u32[]{:S(2)}, u32[]{:S(2)}) %all-to-all-start.2) | async-done | bytes 262176 | tf_op jit(solution)/shard_map/all_to_all | solution.py:210
  232.1 0.9 broadcast_select_fusion
  233.0 85.8 %all-reduce.11.cloned.1.call-done = bf16[64,4,512]{2,1,0:T(4,128)(2,1)} async-done(((bf16[64,4,512]{2,1,0:T(4,128)(2,1)}), bf16[64,4,512]{2,1,0:T(4,128)(2,1)}) %all-reduce.11.cloned.1.call-update) | async-done | bytes 262160
  318.8 1.3 constant_dynamic-slice_fusion
  (164 shorter events, 22.0 us)
Async XLA Ops:
  7.2 127.0 %copy-start = (bf16[96,512]{1,0:T(8,128)(2,1)S(1)}, bf16[96,512]{1,0:T(8,128)(2,1)}, u32[]{:S(2)}) copy-start(bf16[96,512]{1,0:T(8,128)(2,1)} %param.37) | copy-start | bytes 294916
  7.2 17.3 %copy-start.18 = (f32[16,512]{1,0:T(8,128)S(1)}, f32[16,512]{1,0:T(8,128)}, u32[]{:S(2)}) copy-start(f32[16,512]{1,0:T(8,128)} %param.30) | copy-start | bytes 98308
  7.2 18.4 %copy-start.17 = (f32[16,8,1024]{2,1,0:T(8,128)S(1)}, f32[16,8,1024]{2,1,0:T(8,128)}, u32[]{:S(2)}) copy-start(f32[16,8,1024]{2,1,0:T(8,128)} %param.29) | copy-start | bytes 1572868
  9.4 16.3 %copy-start.23 = (pred[16]{0:T(512)(128)(4,1)}, pred[16]{0:T(512)(128)(4,1)S(1)}, u32[]{:S(2)}) copy-start(pred[16]{0:T(512)(128)(4,1)S(1)} %get-tuple-element.18) | copy-start | bytes 52
  9.4 16.3 %copy-start.21 = (s32[1024]{0:T(1024)}, s32[1024]{0:T(1024)S(1)}, u32[]{:S(2)}) copy-start(s32[1024]{0:T(1024)S(1)} %pad_clamp_fusion.1) | copy-start | bytes 12292
  18.0 13.0 %all-to-all-start.3 = ((bf16[2,8,512]{2,1,0:T(8,128)(2,1)}), bf16[2,8,512]{2,1,0:T(8,128)(2,1)S(1)}, u32[]{:S(2)}, u32[]{:S(2)}) async-start(bf16[2,8,512]{2,1,0:T(8,128)(2,1)} %fusion.67), calls=%async_computation.3 | async-start | bytes 32768 | tf_op jit(solution)/shard_map/all_to_all | solution.py:217
  21.8 151.8 %copy-start.19 = (pred[16]{0:T(512)(128)(4,1)}, pred[16]{0:T(512)(128)(4,1)S(1)}, u32[]{:S(2)}) copy-start(pred[16]{0:T(512)(128)(4,1)S(1)} %get-tuple-element.64) | copy-start | bytes 52
  23.3 11.6 %copy-start.25 = (pred[16]{0:T(512)(128)(4,1)}, pred[16]{0:T(512)(128)(4,1)S(1)}, u32[]{:S(2)}) copy-start(pred[16]{0:T(512)(128)(4,1)S(1)} %get-tuple-element.16) | copy-start | bytes 52
  25.7 2.8 copy-start.36
  25.7 3.4 %copy-start.35 = (u32[32]{0:T(128)S(1)}, u32[32]{0:T(128)}, u32[]{:S(2)}) copy-start(u32[32]{0:T(128)} %constant.160) | copy-start | bytes 388
  25.7 4.0 %copy-start.16 = (bf16[8,16,2048]{2,1,0:T(8,128)(2,1)S(1)}, bf16[8,16,2048]{2,1,0:T(8,128)(2,1)}, u32[]{:S(2)}) copy-start(bf16[8,16,2048]{2,1,0:T(8,128)(2,1)} %param.43) | copy-start | bytes 1572868
  28.5 9.7 %copy-start.22 = (s32[1024]{0:T(1024)}, s32[1024]{0:T(1024)S(1)}, u32[]{:S(2)}) copy-start(s32[1024]{0:T(1024)S(1)} %pad_clamp_fusion) | copy-start | bytes 12292
  31.0 7.2 %all-to-all-start.1 = ((f32[2,8,512]{2,1,0:T(8,128)}), f32[2,8,512]{2,1,0:T(8,128)S(1)}, u32[]{:S(2)}, u32[]{:S(2)}) async-start(f32[2,8,512]{2,1,0:T(8,128)} %select_bitcast_fusion.1), calls=%async_computation.1 | async-start | bytes 65536 | tf_op jit(solution)/shard_map/all_to_all | solution.py:177
  35.6 10.1 %copy-start.28 = (bf16[512,96]{0,1:T(8,128)(2,1)S(1)}, bf16[512,96]{0,1:T(8,128)(2,1)}, u32[]{:S(2)}) copy-start(bf16[512,96]{0,1:T(8,128)(2,1)} %param.36) | copy-start | bytes 294916
  35.6 10.3 %copy-start.29 = (bf16[512,96]{0,1:T(8,128)(2,1)S(1)}, bf16[512,96]{0,1:T(8,128)(2,1)}, u32[]{:S(2)}) copy-start(bf16[512,96]{0,1:T(8,128)(2,1)} %param.33) | copy-start | bytes 294916
  38.2 36.3 %all-to-all-start = ((f32[16,8,1024]{2,1,0:T(8,128)}), f32[16,8,1024]{2,1,0:T(8,128)S(1)}, u32[]{:S(2)}, u32[]{:S(2)}) async-start(f32[16,8,1024]{2,1,0:T(8,128)} %broadcast_select_fusion.2), calls=%async_computation | async-start | bytes 1048576 | tf_op jit(solution)/shard_map/all_to_all | solution.py:174
  41.7 92.4 %all-reduce.13.cloned.1.call-start = ((), (), s32[]{:S(2)}) async-start(), calls=%async_computation.5 | async-start | bytes 2883584 | tf_op jit(solution)/shard_map/psum | solution.py:80
  44.4 24.1 %copy-start.30 = (bf16[96,512]{1,0:T(8,128)(2,1)S(1)}, bf16[96,512]{1,0:T(8,128)(2,1)}, u32[]{:S(2)}) copy-start(bf16[96,512]{1,0:T(8,128)(2,1)} %param.34) | copy-start | bytes 294916
  44.4 24.1 %copy-start.31 = (f32[512]{0:T(512)S(1)}, f32[512]{0:T(512)}, u32[]{:S(2)}) copy-start(f32[512]{0:T(512)} %param.35) | copy-start | bytes 6148
  69.7 1.3 copy-start.12
  69.7 1.3 copy-start.13
  69.7 2.4 copy-start.14
  69.7 3.6 %copy-start.15 = (f32[16,8,64]{2,1,0:T(8,128)}, f32[16,8,64]{2,1,0:T(8,128)S(1)}, u32[]{:S(2)}) copy-start(f32[16,8,64]{2,1,0:T(8,128)S(1)} %get-tuple-element.35) | copy-start | bytes 98308
  75.1 59.1 %copy-start.32 = (f32[512]{0:T(512)S(1)}, f32[512]{0:T(512)}, u32[]{:S(2)}) copy-start(f32[512]{0:T(512)} %param.39) | copy-start | bytes 6148
  75.1 59.0 %copy-start.33 = (f32[512]{0:T(512)S(1)}, f32[512]{0:T(512)}, u32[]{:S(2)}) copy-start(f32[512]{0:T(512)} %param.40) | copy-start | bytes 6148
  75.1 59.0 %copy-start.34 = (f32[512]{0:T(512)S(1)}, f32[512]{0:T(512)}, u32[]{:S(2)}) copy-start(f32[512]{0:T(512)} %param.38) | copy-start | bytes 6148
  134.2 3.1 copy-start.7
  134.2 3.8 %copy-start.27 = (f32[8,64]{1,0:T(8,128)S(1)}, f32[8,64]{1,0:T(8,128)}, u32[]{:S(2)}) copy-start(f32[8,64]{1,0:T(8,128)} %param.41) | copy-start | bytes 6148
  147.9 2.4 copy-start.1
  156.6 2.4 copy-start.2
  164.6 4.6 %copy-start.3 = (f32[16,8,16,64]{3,2,1,0:T(8,128)S(1)}, f32[16,8,16,64]{3,2,1,0:T(8,128)}, u32[]{:S(2)}) copy-start(f32[16,8,16,64]{3,2,1,0:T(8,128)} %get-tuple-element.55) | copy-start | bytes 1572868
  169.1 4.5 %copy-start.8 = (f32[16,1,8,16]{3,2,0,1:T(8,128)}, f32[16,1,8,16]{3,2,0,1:T(8,128)S(1)}, u32[]{:S(2)}) copy-start(f32[16,1,8,16]{3,2,0,1:T(8,128)S(1)} %get-tuple-element.75) | copy-start | bytes 24580
  169.1 4.5 %copy-start.9 = (f32[16,1,8,16]{3,2,0,1:T(8,128)}, f32[16,1,8,16]{3,2,0,1:T(8,128)S(1)}, u32[]{:S(2)}) copy-start(f32[16,1,8,16]{3,2,0,1:T(8,128)S(1)} %get-tuple-element.76) | copy-start | bytes 24580
  173.5 42.4 %copy-start.4 = (f32[16,8,16,64]{3,2,1,0:T(8,128)S(1)}, f32[16,8,16,64]{3,2,1,0:T(8,128)}, u32[]{:S(2)}) copy-start(f32[16,8,16,64]{3,2,1,0:T(8,128)} %get-tuple-element.56) | copy-start | bytes 1572868
  173.6 0.6 copy-start.10
  173.6 0.6 copy-start.11
  215.9 2.2 copy-start.20
  217.0 1.1 copy-start.5
  217.0 1.2 copy-start.6
  218.2 3.7 %copy-start.24 = (pred[16]{0:T(512)(128)(4,1)S(1)}, pred[16]{0:T(512)(128)(4,1)}, u32[]{:S(2)}) copy-start(pred[16]{0:T(512)(128)(4,1)} %copy-done.23) | copy-start | bytes 52
  222.7 8.6 %all-to-all-start.2 = ((bf16[16,8,1024]{2,1,0:T(8,128)(2,1)}), bf16[16,8,1024]{2,1,0:T(8,128)(2,1)S(1)}, u32[]{:S(2)}, u32[]{:S(2)}) async-start(bf16[16,8,1024]{2,1,0:T(8,128)(2,1)} %select_convert_fusion), calls=%async_computation.2 | async-start | bytes 524288 | tf_op jit(solution)/shard_map/all_to_all | solution.py:210
  226.2 92.6 %all-reduce.11.cloned.1.call-start = ((), (), s32[]{:S(2)}) async-start(), calls=%async_computation.4 | async-start | bytes 524288
  226.2 5.9 %copy-start.26 = (pred[16]{0:T(512)(128)(4,1)S(1)}, pred[16]{0:T(512)(128)(4,1)}, u32[]{:S(2)}) copy-start(pred[16]{0:T(512)(128)(4,1)} %copy-done.25) | copy-start | bytes 52
Sparse Core Ops, SparseCore 0:
  69.8 64.3 all-reduce.12
  230.4 88.3 all-reduce.10
where the time goes:
time: 329 us; the launch traced here: 327 us
  waiting for transfers between devices  151 us (46%)
  blocking collectives  62.1 us (19%)
  other arithmetic  38.9 us (12%)
  local copies, waits for them, and re-layouts  38.2 us (12%)
  between operations  15.5 us (5%)
  starting transfers between devices  13.5 us (4%)
  matrix products  7.72 us (2%)
    unnamed x3, waiting for transfers between devices  85.8 us
    psum x1, waiting for transfers between devices, time_mix(): lax.psum((recept_part, key_part, decay_part, learn_part), 'row')  58.6 us
    psum x1, blocking collectives, time_mix(): lax.psum((recept_part, key_part, decay_part, learn_part), 'row')  20.6 us
    mul x4, other arithmetic, time_mix(): removed[..., None]  19 us
    psum x1, blocking collectives, time_mix(): head_sum = lax.psum(jnp.sum(groupwise_results, axis=-1), 'row')  17.7 us
    psum x1, blocking collectives, time_mix(): lax.psum(jnp.sum(offset * offset, axis=-1), 'row') / CHANNEL_SPAN  17.4 us
    mul x6, local copies, waits for them, and re-layouts, time_mix(): payload_entries[:, position][..., None]  9.83 us
    dot_general x7, matrix products, project(): jnp.einsum('rtd,de->rte', token_rows, weight, preferred_element_type=jnp....  7.46 us
  transfers between devices with their start and end apart: 6, of which 4 were waited for; matrix products, arithmetic and copies ran while one was open for 8% of the time, Pallas kernels for 0%

commit v1 on v0

v1 whole, which is shorter than its diff:
```python
import functools

import jax
import jax.numpy as jnp
from jax import lax
from jax.experimental import pallas as pl
from jax.experimental.pallas import tpu as pltpu
from jax.sharding import PartitionSpec as P

SPAN = 64
TS = 4
F32 = jnp.float32
BF16 = jnp.bfloat16
MESH = pl.DeviceIdType.MESH


def dot(a, b):
    return jnp.dot(a, b, preferred_element_type=F32)


def dot_split(a, ones):
    high = a.astype(BF16)
    low = (a - high.astype(F32)).astype(BF16)
    return dot(high, ones) + dot(low, ones)


def iota2(shape):
    return (
        lax.broadcasted_iota(jnp.int32, shape, 0),
        lax.broadcasted_iota(jnp.int32, shape, 1),
    )


def as_ones(condition):
    return jnp.where(condition, 1.0, 0.0).astype(BF16)


def kernel(
    sizes,
    valid_ref, slot_ref, inv_ref,
    x_ref, pages_hbm, shift_ref, blend_ref, w_hbm, fn_ref, fw_ref, fo_ref,
    cn_ref, cw_ref, co_ref, eg_ref, ac_ref, rc_ref, gg_ref, fp_hbm,
    mixed_ref, state_out, shift_out,
    w_ref, pages_ref, fp_ref,
    x_all, shift_all, pack_out, pack_in, xs_ref, sh_ref, n_ref,
    part_send, part_recv, v_send, v_recv, sum_send, sum_all,
    r_d, kd_d, kl_d, ka_d, dec_d, s_ref, read_ref,
    back_out, back_in, last_all,
    stat_send, stat_recv, out_send, out_recv, fin_send, fin_recv,
    local_sem,
    sx, rx, ssh, rsh, spg, rpg, spt, rpt, sv, rv, ssm, rsm, sst, rst,
    so, ro, sf, rf, sbk, rbk, sla, rla,
):
    R, H, Z = sizes
    RD = pages_ref.shape[0]
    TOK = RD * TS
    BT = TOK // H
    ZT = TOK // Z
    DL = fn_ref.shape[1]
    me_r, me_h, me_z = lax.axis_index("req"), lax.axis_index("head"), lax.axis_index("row")
    pending = []

    def peer(axis, d):
        me, n = {"req": (me_r, R), "head": (me_h, H), "row": (me_z, Z)}[axis]
        return lax.rem(me + d, n)

    def send(src, dst, ssem, rsem, axis, d):
        c = pltpu.make_async_remote_copy(
            src_ref=src, dst_ref=dst, send_sem=ssem.at[d - 1], recv_sem=rsem.at[d - 1],
            device_id={axis: peer(axis, d)}, device_id_type=MESH,
        )
        c.start()
        pending.append(c)
        return c

    loads = [
        pltpu.make_async_copy(pages_hbm, pages_ref, local_sem.at[0]),
        pltpu.make_async_copy(w_hbm, w_ref, local_sem.at[1]),
        pltpu.make_async_copy(fp_hbm, fp_ref, local_sem.at[2]),
    ]
    for c in loads:
        c.start()

    barrier = pltpu.get_barrier_semaphore()
    for axis, n in (("req", R), ("head", H), ("row", Z)):
        for d in range(1, n):
            pl.semaphore_signal(barrier, inc=1, device_id={axis: peer(axis, d)}, device_id_type=MESH)
    pl.semaphore_wait(barrier, R + H + Z - 3)

    xc = [send(x_ref, x_all.at[me_h], sx, rx, "head", d) for d in range(1, H)]
    shc = [send(shift_ref, shift_all.at[pl.ds(me_r * RD, RD)], ssh, rsh, "req", d) for d in range(1, R)]
    x_all[me_h] = x_ref[...]
    shift_all[pl.ds(pl.multiple_of(me_r * RD, RD), RD), :] = shift_ref[...]

    loads[0].wait()
    for p in range(RD):
        page = pages_ref[p]
        half = page.shape[1] // 2
        pack_out[p] = jnp.concatenate([page[:, :half], page[:, half:]], axis=0).astype(BF16)
    pgc = [send(pack_out, pack_in.at[pl.ds(me_r * RD, RD)], spg, rpg, "req", d) for d in range(1, R)]

    row, col = iota2((512, 512))
    same_head = as_ones((row >> 6) == (col >> 6))
    to_rows = as_ones(
        (((row >> 4) & 3) == (col >> 7)) & ((row >> 6) == ((col >> 4) & 7)) & ((row & 15) == (col & 15))
    )
    row, col = iota2((512, 128))
    head_to_feature = as_ones((row >> 6) == (col >> 4))
    row, col = iota2((128, 128))
    half_sum = as_ones((row >> 6) == (col >> 6))
    parity_sum = as_ones((row >> 6) == (col & 1))
    block16 = as_ones((row >> 4) == (col >> 4))
    row, col = iota2((128, 1024))
    spread = as_ones((row & 15) == (col >> 6))
    for r in range(RD):
        n_ref[pl.ds(TS * r, TS), :] = jnp.full((TS, 128), valid_ref[me_r * RD + r], jnp.int32)
    trow, _ = iota2((TOK, 128))
    live = n_ref[...] > (trow & 3)
    live1 = live[:, :1]

    for c in xc + shc:
        c.wait_recv()
    current = x_all[...].reshape(TOK, x_all.shape[2]).astype(F32)
    xs_ref[...] = current
    for r in range(RD):
        sh_ref[pl.ds(TS * r, 1), :] = shift_all[pl.ds(slot_ref[me_r * RD + r], 1), :]
    wide, _ = iota2(current.shape)
    before = jnp.where((wide & 3) == 0, sh_ref[...], pltpu.roll(current, 1, 0))
    towards = before - current
    mixed_in = [(current + towards * blend_ref[b : b + 1, :]).astype(BF16) for b in range(5)]
    d_part = dot(mixed_in[1], fn_ref[...])
    l_part = dot(mixed_in[4], cn_ref[...])
    loads[1].wait()
    r_part = dot(mixed_in[0], w_ref[0])
    k_part = dot(mixed_in[2], w_ref[1])
    fill = jnp.zeros((TOK, 128 - DL), F32)
    part = jnp.concatenate([r_part, k_part, d_part, fill, l_part, fill], axis=1)
    part_send[...] = part.astype(BF16).reshape(part_send.shape)
    ptc = [send(part_send.at[peer("row", d)], part_recv.at[d - 1], spt, rpt, "row", d) for d in range(1, Z)]
    v_part = dot(dot(mixed_in[3], w_ref[2]).astype(BF16), to_rows)
    for q in range(Z):
        v_send[q] = v_part[:, 128 * q : 128 * (q + 1)].astype(BF16)
    vc = [send(v_send.at[peer("row", d)], v_recv.at[d - 1], sv, rv, "row", d) for d in range(1, Z)]

    base = pl.multiple_of(me_r * RD, RD)
    for r in range(RD):
        last_all[pl.ds(base + r, 1), :] = xs_ref[pl.ds(TS * r + jnp.clip(valid_ref[me_r * RD + r] - 1, 0, TS - 1), 1), :]
    lac = [
        send(last_all.at[pl.ds(base, RD)], last_all.at[pl.ds(base, RD)], sla, rla, "req", d)
        for d in range(1, R)
    ]

    total = part_send[me_z].astype(F32)
    for d in range(1, Z):
        ptc[d - 1].wait_recv()
        total = total + part_recv[d - 1].astype(F32)
    sum_send[...] = total.astype(BF16)
    smc = [send(sum_send, sum_all.at[me_z], ssm, rsm, "row", d) for d in range(1, Z)]
    sum_all[me_z] = sum_send[...]

    for c in pgc:
        c.wait_recv()
    for r in range(RD):
        page = slot_ref[me_r * RD + r]
        here = page - me_r * RD
        mine = jnp.logical_and(here >= 0, here < RD)
        own = pages_ref[jnp.clip(here, 0, RD - 1)]
        got = pack_in[page].astype(F32)
        for j in range(8):
            away = got[8 * (j >> 2) : 8 * (j >> 2) + 8, 128 * (j & 3) : 128 * (j & 3) + 128]
            s_ref[j, r] = jnp.where(mine, own[:, 128 * j : 128 * j + 128], away)

    values = v_send[me_z].astype(F32)
    for d in range(1, Z):
        vc[d - 1].wait_recv()
        values = values + v_recv[d - 1].astype(F32)

    for c in smc:
        c.wait_recv()
    sums = sum_all[...].reshape(TOK, sum_all.shape[2]).astype(F32)
    query, key_vec = sums[:, :512], sums[:, 512:1024]
    decay_low = jnp.tanh(sums[:, 1024 : 1024 + DL]).astype(BF16)
    learn_low = sums[:, 1152 : 1152 + DL].astype(BF16)
    z = fo_ref[...] + dot(decay_low, fw_ref[...])
    decay = jnp.exp(-0.6065306597126334 / (1.0 + jnp.exp(-z)))
    y = co_ref[...] + dot(learn_low, cw_ref[...])
    learn = 1.0 / (1.0 + jnp.exp(-y))
    scaled = key_vec * eg_ref[...]
    squares = dot((scaled * scaled).astype(BF16), same_head)
    key_dir = scaled * lax.rsqrt(squares + 1e-6)
    key_adj = key_vec * (1.0 + (learn - 1.0) * ac_ref[...])
    bonus = jnp.where(
        live, dot((query * key_adj * rc_ref[...]).astype(BF16), head_to_feature) * values, 0.0
    )
    lane = lax.broadcasted_iota(jnp.int32, (TOK, 128), 1)
    low_half = lane < 64

    def heads_out(ref, a):
        for p in range(4):
            pair = a[:, 128 * p : 128 * p + 128]
            other = pltpu.roll(pair, 64, 1)
            ref[pl.ds(2 * p, TOK, stride=8), :] = jnp.where(low_half, pair, other)
            ref[pl.ds(2 * p + 1, TOK, stride=8), :] = jnp.where(low_half, other, pair)

    heads_out(r_d, jnp.where(live1, query, 0.0))
    heads_out(kd_d, key_dir)
    heads_out(kl_d, jnp.where(live1, -key_dir * learn, 0.0))
    heads_out(ka_d, jnp.where(live1, key_adj, 0.0))
    heads_out(dec_d, jnp.where(live1, decay, 1.0))

    srow, scol = iota2((8, 128))
    own_head = (scol >> 4) == srow
    values3 = values.reshape(RD, TS, 128)
    for t in range(TS):
        kd, kl, ka, dec, rq = (
            ref[...].reshape(RD, TS, 8, 128)[:, t] for ref in (kd_d, kl_d, ka_d, dec_d, r_d)
        )
        vt = jnp.where(own_head[None], jnp.broadcast_to(values3[:, t][:, None, :], (RD, 8, 128)), 0.0)
        v_wide = dot(vt.reshape(RD * 8, 128).astype(BF16), spread)
        now = [s_ref[j] for j in range(8)]
        hit = dot(
            jnp.concatenate([(s * kd).reshape(RD * 8, 128).astype(BF16) for s in now], axis=0), half_sum
        )
        after = []
        for j in range(8):
            removed = hit[128 * j : 128 * j + 128].reshape(RD, 8, 128)
            vj = v_wide[:, 128 * j : 128 * j + 128].reshape(RD, 8, 128)
            s = now[j] * dec + removed * kl + vj * ka
            s_ref[j] = s
            after.append((s * rq).reshape(RD * 8, 128).astype(BF16))
        seen = dot(jnp.concatenate(after, axis=0), parity_sum)
        acc = jnp.zeros((RD, 8, 128), F32)
        for j in range(8):
            pick = own_head & (((scol & 15) >> 1) == j)
            acc = acc + jnp.where(pick[None], seen[128 * j : 128 * j + 128].reshape(RD, 8, 128), 0.0)
        read_ref[pl.ds(t, RD, stride=TS), :] = jnp.sum(acc, axis=1)

    reading = read_ref[...]
    vrows = 16
    mean_own = dot_split(reading, block16) * (1.0 / vrows)
    off = reading - mean_own
    sq_own = dot_split(off * off, block16)
    is_mean = (lane & 8) == 0
    slot_here = (lane & 7) == (trow & 7)
    packed = jnp.where(slot_here, jnp.where(is_mean, mean_own, sq_own), 0.0)
    stat_send[...] = jnp.sum(packed.reshape(TOK // 8, 8, 128), axis=1)
    stc = [send(stat_send, stat_recv.at[d - 1], sst, rst, "row", d) for d in range(1, Z)]

    for r in range(RD):
        lo = jnp.concatenate([s_ref[j, r] for j in range(4)], axis=1)
        hi = jnp.concatenate([s_ref[j, r] for j in range(4, 8)], axis=1)
        back_out[r] = jnp.concatenate([lo, hi], axis=0).astype(BF16)
    bkc = [send(back_out, back_in.at[pl.ds(me_r * RD, RD)], sbk, rbk, "req", d) for d in range(1, R)]

    packs = [stat_send[...]]
    for d in range(1, Z):
        stc[d - 1].wait_recv()
        packs.append(stat_recv[d - 1])
    both = sum(packs)
    center = both * (1.0 / Z)
    between = sum([(p - center) * (p - center) for p in packs]) * vrows
    spread_all = (both + pltpu.roll(between, 8, 1)) * (1.0 / (vrows * Z))
    _, plane = iota2(both.shape)
    both = jnp.where((plane & 8) == 0, center, lax.rsqrt(spread_all + 64e-5))
    both = jnp.broadcast_to(both[:, None, :], (TOK // 8, 8, 128)).reshape(TOK, 128)
    mean = dot_split(jnp.where(slot_here & is_mean, both, 0.0), block16)
    scale = dot_split(jnp.where(slot_here & jnp.logical_not(is_mean), both, 0.0), block16)
    normed = ((reading - mean) * scale * gg_ref[...] + bonus).astype(BF16)

    loads[2].wait()
    for q in range(Z):
        block = dot(normed, fp_ref[:, 512 * q : 512 * (q + 1)]).astype(BF16)
        for b in range(H):
            out_send[b, q] = block[BT * b : BT * (b + 1)]
    oc = [send(out_send.at[peer("head", d)], out_recv.at[d - 1], so, ro, "head", d) for d in range(1, H)]

    for c in bkc + lac:
        c.wait_recv()
    for p in range(RD):
        q = inv_ref[me_r * RD + p]
        here = q - me_r * RD
        mine = jnp.logical_and(here >= 0, here < RD)
        at = jnp.clip(here, 0, RD - 1)
        got = back_in[q].astype(F32)
        for j in range(8):
            away = got[8 * (j >> 2) : 8 * (j >> 2) + 8, 128 * (j & 3) : 128 * (j & 3) + 128]
            state_out[p, :, 128 * j : 128 * j + 128] = jnp.where(mine, s_ref[j, at], away)
        shift_out[pl.ds(p, 1), :] = last_all[pl.ds(q, 1), :]

    acc = out_send[me_h].astype(F32)
    for d in range(1, H):
        oc[d - 1].wait_recv()
        acc = acc + out_recv[d - 1].astype(F32)
    fin_send[...] = acc.astype(BF16)
    fc = [send(fin_send.at[peer("row", d)], fin_recv.at[d - 1], sf, rf, "row", d) for d in range(1, Z)]
    res = fin_send[me_z].astype(F32)
    for d in range(1, Z):
        fc[d - 1].wait_recv()
        res = res + fin_recv[d - 1].astype(F32)
    mixed_ref[...] = res.astype(BF16)
    for c in pending:
        c.wait_send()


def per_device(x, valid, slots, pages, shift, blend, w, fn, fw, fo, cn, cw, co, eg, ac, rc, gg, fp):
    R, H, Z = lax.axis_size("req"), lax.axis_size("head"), lax.axis_size("row")
    RD, heads, flat = pages.shape
    wide = shift.shape[1]
    TOK = RD * TS
    BT, ZT = TOK // H, TOK // Z
    everyone = jnp.arange(slots.shape[0], dtype=jnp.int32)
    inv = jnp.sum(jnp.where(slots[None, :] == everyone[:, None], everyone[None, :], 0), axis=1)
    feats = gg.shape[0] * gg.shape[1]
    cols = w.shape[2]
    sums = 2 * cols + 256
    smem = pl.BlockSpec(memory_space=pltpu.SMEM)
    vm = pl.BlockSpec(memory_space=pltpu.VMEM)
    hbm = pl.BlockSpec(memory_space=pl.ANY)
    V = pltpu.VMEM
    sems = []
    for n in (H, R, R, Z, Z, Z, Z, H, Z, R, R):
        sems += [pltpu.SemaphoreType.DMA((max(n - 1, 1),))] * 2
    scratch = [
        V(w.shape, BF16), V(pages.shape, F32), V((feats, fp.shape[2]), BF16),
        V((H, BT, wide), BF16), V((R * RD, wide), F32),
        V((RD, 2 * heads, flat // 2), BF16), V((R * RD, 2 * heads, flat // 2), BF16),
        V((TOK, wide), F32), V((TOK, wide), F32), V((TOK, 128), jnp.int32),
        V((Z, ZT, sums), BF16), V((Z - 1, ZT, sums), BF16),
        V((Z, TOK, feats), BF16), V((Z - 1, TOK, feats), BF16),
        V((ZT, sums), BF16), V((Z, ZT, sums), BF16),
        V((TOK * 8, 128), F32), V((TOK * 8, 128), F32), V((TOK * 8, 128), F32),
        V((TOK * 8, 128), F32), V((TOK * 8, 128), F32),
        V((8, RD, 8, 128), F32), V((TOK, 128), F32),
        V((RD, 2 * heads, flat // 2), BF16), V((R * RD, 2 * heads, flat // 2), BF16),
        V((R * RD, wide), F32),
        V((TOK // 8, 128), F32), V((Z - 1, TOK // 8, 128), F32),
        V((H, Z, BT, wide), BF16), V((H - 1, Z, BT, wide), BF16),
        V((Z, BT, wide), BF16), V((Z - 1, BT, wide), BF16),
        pltpu.SemaphoreType.DMA((3,)),
    ] + sems
    mixed, new_state, new_shift = pl.pallas_call(
        functools.partial(kernel, (R, H, Z)),
        out_shape=(
            jax.ShapeDtypeStruct((BT, wide), BF16),
            jax.ShapeDtypeStruct(pages.shape, F32),
            jax.ShapeDtypeStruct(shift.shape, F32),
        ),
        in_specs=[smem] * 3 + [vm, hbm, vm, vm, hbm] + [vm] * 10 + [hbm],
        out_specs=(vm, vm, vm),
        scratch_shapes=scratch,
        compiler_params=pltpu.CompilerParams(
            collective_id=0, has_side_effects=True, vmem_limit_bytes=50 * 1024 * 1024
        ),
    )(
        valid, slots, inv, x.reshape(BT, wide), pages, shift, blend, w, fn, fw,
        fo.reshape(1, -1), cn, cw, co.reshape(1, -1), eg.reshape(1, -1), ac.reshape(1, -1),
        rc.reshape(1, -1), gg.reshape(1, -1), fp.reshape(feats, -1),
    )
    return mixed.reshape(x.shape), new_state, new_shift


def solution(mesh):
    placed = (
        P(("req", "head"), None, "row"),
        P(),
        P(),
        P("req", "head", "row"),
        P("req", "row"),
        P(None, "row"),
        P(None, "row", "head"),
        P("row", None),
        P(None, "head"),
        P("head"),
        P("row", None),
        P(None, "head"),
        P("head"),
        P("head"),
        P("head"),
        P("head", None),
        P("head", "row"),
        P("head", "row", None),
    )
    return jax.shard_map(
        per_device,
        mesh=mesh,
        in_specs=placed,
        out_specs=(P(("req", "head"), None, "row"), P("req", "head", "row"), P("req", "row")),
        check_vma=False,
    )
```

time: 329 us -> 54.8 us (0.17)
  waiting for transfers between devices: 151 us -> 0 us
  blocking collectives: 62.1 us -> 0 us
  other arithmetic: 38.9 us -> 0.77 us
  Pallas kernels: 0 us -> 35.5 us
  local copies, waits for them, and re-layouts: 38.2 us -> 17.1 us
  between operations: 15.5 us -> 0.68 us
  starting transfers between devices: 13.5 us -> 0 us
  matrix products: 7.72 us -> 0 us
    unnamed x3 -> x0, waiting for transfers between devices: 85.8 us -> none
    psum x1 -> x0, waiting for transfers between devices: 58.6 us -> none  [time_mix(): lax.psum((recept_part, key_part, decay_part, learn_part), 'row')]
    psum x3 -> x0, blocking collectives: 55.6 us -> none  [the longest x1 20.6 us: time_mix(): lax.psum((recept_part, key_part, decay_part, learn_part), 'row')]
    pallas_call x0 -> x1, Pallas kernels: none -> 35.5 us  [per_device(): pl.pallas_call(functools.partial(kernel, (R, H, Z)), out_shape=(jax.Shape...]
    mul x20 -> x0, local copies, waits for them, and re-layouts: 19.7 us -> none  [the longest x6 9.83 us: time_mix(): payload_entries[:, position][..., None]]
    mul x5 -> x0, other arithmetic: 19.7 us -> none  [the longest x4 19 us: time_mix(): removed[..., None]]
    all_to_all x4 -> x0, starting transfers between devices: 13.4 us -> none  [the longest x1 3.49 us: per_device(): lax.all_to_all(pick_rows(memory_sheets, leaving), 'req', split_axis=0, co...]
    unnamed x79 -> x30, local copies, waits for them, and re-layouts: 5 us -> 14.2 us
  transfers between devices with their start and end apart: 6 -> 0, of which waited for: 4 -> 0; matrix products, arithmetic and copies ran while one was open for 8% -> 0% of each run, Pallas kernels for 0% -> 0%
where the time goes in v1:
time: 54.8 us; the launch traced here: 54.1 us
  Pallas kernels  35.5 us (65%)
  local copies, waits for them, and re-layouts  17.1 us (31%)
  other arithmetic  0.77 us (1%)
  between operations  0.68 us (1%)
    pallas_call x1, Pallas kernels, per_device(): pl.pallas_call(functools.partial(kernel, (R, H, Z)), out_shape=(jax.Shape...  35.5 us
    unnamed x30, local copies, waits for them, and re-layouts  14.2 us

profile of v1, /device:TPU:0, one launch (start us, length us, event | category | flops | bytes accessed | tf_op | source)
XLA Modules:
  0.0 54.1 jit_solution(10897368902609746323)
XLA Ops:
  0.6 0.8 %reshape.40.gg_ref = f32[1,128]{1,0:T(1,128)S(1)} reshape(f32[8,16]{1,0:T(8,128)} %param.34) | data formatting | bytes 1024 | tf_op jit(solution)/shard_map/reshape | solution.py:357
  1.4 0.8 %select_reduce_fusion.inv_ref = s32[32]{0:T(128)S(1)} fusion(s32[32]{0:T(128)} %slot_ref.1), kind=kLoop, calls=%fused_computation | loop fusion | flops 3040 | bytes 256 | tf_op jit(solution)/shard_map/reduce_sum | solution.py:312
  2.2 0.8 %reshape.39.rc_ref = f32[1,512]{1,0:T(1,128)S(1)} reshape(f32[8,64]{1,0:T(8,128)} %param.33) | data formatting | bytes 4096 | tf_op jit(solution)/shard_map/reshape | solution.py:357
  2.9 0.7 %reshape.34.x_ref = bf16[16,512]{1,0:T(8,128)(2,1)S(1)} reshape(bf16[4,4,512]{2,1,0:T(4,128)(2,1)} %param.18) | data formatting | bytes 32768 | tf_op jit(solution)/shard_map/reshape | solution.py:355
  3.7 1.0 %copy.23.fn_ref = bf16[512,96]{1,0:T(8,128)(2,1)S(1)} copy(bf16[512,96]{0,1:T(8,128)(2,1)} %param.25) | data formatting | bytes 196608 | tf_op args[7]
  4.7 1.0 %copy.24.cn_ref = bf16[512,96]{1,0:T(8,128)(2,1)S(1)} copy(bf16[512,96]{0,1:T(8,128)(2,1)} %param.28) | data formatting | bytes 196608 | tf_op args[10]
  5.7 0.0 copy-start
  5.7 1.4 %copy-done = bf16[3,512,512]{2,1,0:T(8,128)(2,1)S(1)} copy-done((bf16[3,512,512]{2,1,0:T(8,128)(2,1)S(1)}, bf16[3,512,512]{2,1,0:T(8,128)(2,1)}, u32[]{:S(2)}) %copy-start) | copy-done | bytes 1572888
  7.1 0.0 copy-start.1
  7.1 1.0 %copy-done.1 = f32[16,8,1024]{2,1,0:T(8,128)S(1)} copy-done((f32[16,8,1024]{2,1,0:T(8,128)S(1)}, f32[16,8,1024]{2,1,0:T(8,128)}, u32[]{:S(2)}) %copy-start.1) | copy-done | bytes 524312
  8.2 0.0 copy-start.2
  8.2 1.0 %copy-done.2 = bf16[8,16,2048]{2,1,0:T(8,128)(2,1)S(1)} copy-done((bf16[8,16,2048]{2,1,0:T(8,128)(2,1)S(1)}, bf16[8,16,2048]{2,1,0:T(8,128)(2,1)}, u32[]{:S(2)}) %copy-start.2) | copy-done | bytes 524312
  9.2 0.0 copy-start.3
  9.2 0.9 %copy-done.3 = bf16[96,512]{1,0:T(8,128)(2,1)S(1)} copy-done((bf16[96,512]{1,0:T(8,128)(2,1)S(1)}, bf16[96,512]{1,0:T(8,128)(2,1)}, u32[]{:S(2)}) %copy-start.3) | copy-done | bytes 98328
  10.1 0.0 copy-start.4
  10.1 0.9 %copy-done.4 = bf16[96,512]{1,0:T(8,128)(2,1)S(1)} copy-done((bf16[96,512]{1,0:T(8,128)(2,1)S(1)}, bf16[96,512]{1,0:T(8,128)(2,1)}, u32[]{:S(2)}) %copy-start.4) | copy-done | bytes 98328
  11.0 0.0 copy-start.5
  11.0 0.8 %copy-done.5 = f32[16,512]{1,0:T(8,128)S(1)} copy-done((f32[16,512]{1,0:T(8,128)S(1)}, f32[16,512]{1,0:T(8,128)}, u32[]{:S(2)}) %copy-start.5) | copy-done | bytes 32792
  11.7 0.0 copy-start.6
  11.7 0.7 %copy-done.6 = f32[5,512]{1,0:T(8,128)S(1)} copy-done((f32[5,512]{1,0:T(8,128)S(1)}, f32[5,512]{1,0:T(8,128)}, u32[]{:S(2)}) %copy-start.6) | copy-done | bytes 10264
  12.5 0.0 copy-start.7
  12.5 0.7 %copy-done.7 = f32[512]{0:T(512)S(1)} copy-done((f32[512]{0:T(512)S(1)}, f32[512]{0:T(512)}, u32[]{:S(2)}) %copy-start.7) | copy-done | bytes 2072
  13.1 0.0 copy-start.8
  13.1 0.7 %copy-done.8 = f32[512]{0:T(512)S(1)} copy-done((f32[512]{0:T(512)S(1)}, f32[512]{0:T(512)}, u32[]{:S(2)}) %copy-start.8) | copy-done | bytes 2072
  13.8 0.0 copy-start.9
  13.8 0.7 %copy-done.9 = f32[512]{0:T(512)S(1)} copy-done((f32[512]{0:T(512)S(1)}, f32[512]{0:T(512)}, u32[]{:S(2)}) %copy-start.9) | copy-done | bytes 2072
  14.5 0.0 copy-start.10
  14.5 0.7 %copy-done.10 = f32[512]{0:T(512)S(1)} copy-done((f32[512]{0:T(512)S(1)}, f32[512]{0:T(512)}, u32[]{:S(2)}) %copy-start.10) | copy-done | bytes 2072
  15.2 0.0 copy-start.11
  15.2 0.7 %copy-done.11 = s32[32]{0:T(128)S(1)} copy-done((s32[32]{0:T(128)S(1)}, s32[32]{0:T(128)}, u32[]{:S(2)}) %copy-start.11) | copy-done | bytes 152
  15.8 0.0 copy-start.12
  15.8 0.7 %copy-done.12 = s32[32]{0:T(128)S(1)} copy-done((s32[32]{0:T(128)S(1)}, s32[32]{0:T(128)}, u32[]{:S(2)}) %copy-start.12) | copy-done | bytes 152
  16.5 35.5 %shard_map.193 = (bf16[16,512]{1,0:T(8,128)(2,1)S(1)}, f32[16,8,1024]{2,1,0:T(8,128)S(1)}, f32[16,512]{1,0:T(8,128)S(1)}) custom-call(s32[32]{0:T(128)S(1)} %copy-done.11, s32[32]{0:T(128)S(1)} %copy-done.12, s32[32]{0:T(128)S(1)} %select_reduce_fusion.inv_ref, bf16[16,512]{1,0:T(8,128)(2,1)S(1)} %reshape.34.x_ref, f32[16,8,1024]{2,1,0:T(8,128)S(1)} %copy-done.1, ...), custom_call_target="tpu_custom_call" | custom-call | tf_op jit(solution)/shard_map/pallas_call | solution.py:341
  52.0 0.6 %reshape.42 = bf16[4,4,512]{2,1,0:T(4,128)(2,1)} reshape(bf16[16,512]{1,0:T(8,128)(2,1)S(1)} %get-tuple-element.6) | data formatting | bytes 32768 | tf_op jit(solution)/shard_map/reshape | solution.py:359
  52.6 0.8 %copy.27 = f32[16,8,1024]{2,1,0:T(8,128)} copy(f32[16,8,1024]{2,1,0:T(8,128)S(1)} %get-tuple-element.13) | data formatting | bytes 1048576
  53.4 0.6 %copy.28 = f32[16,512]{1,0:T(8,128)} copy(f32[16,512]{1,0:T(8,128)S(1)} %get-tuple-element.14) | data formatting | bytes 65536
Async XLA Ops:
  5.7 1.4 %copy-start = (bf16[3,512,512]{2,1,0:T(8,128)(2,1)S(1)}, bf16[3,512,512]{2,1,0:T(8,128)(2,1)}, u32[]{:S(2)}) copy-start(bf16[3,512,512]{2,1,0:T(8,128)(2,1)} %w_hbm.1) | copy-start | bytes 4718596
  7.1 1.0 %copy-start.1 = (f32[16,8,1024]{2,1,0:T(8,128)S(1)}, f32[16,8,1024]{2,1,0:T(8,128)}, u32[]{:S(2)}) copy-start(f32[16,8,1024]{2,1,0:T(8,128)} %pages_hbm.1) | copy-start | bytes 1572868
  8.2 1.0 %copy-start.2 = (bf16[8,16,2048]{2,1,0:T(8,128)(2,1)S(1)}, bf16[8,16,2048]{2,1,0:T(8,128)(2,1)}, u32[]{:S(2)}) copy-start(bf16[8,16,2048]{2,1,0:T(8,128)(2,1)} %param.35) | copy-start | bytes 1572868
  9.2 0.9 %copy-start.3 = (bf16[96,512]{1,0:T(8,128)(2,1)S(1)}, bf16[96,512]{1,0:T(8,128)(2,1)}, u32[]{:S(2)}) copy-start(bf16[96,512]{1,0:T(8,128)(2,1)} %fw_ref.1) | copy-start | bytes 294916
  10.1 0.9 %copy-start.4 = (bf16[96,512]{1,0:T(8,128)(2,1)S(1)}, bf16[96,512]{1,0:T(8,128)(2,1)}, u32[]{:S(2)}) copy-start(bf16[96,512]{1,0:T(8,128)(2,1)} %cw_ref.1) | copy-start | bytes 294916
  11.0 0.8 %copy-start.5 = (f32[16,512]{1,0:T(8,128)S(1)}, f32[16,512]{1,0:T(8,128)}, u32[]{:S(2)}) copy-start(f32[16,512]{1,0:T(8,128)} %shift_ref.1) | copy-start | bytes 98308
  11.7 0.7 %copy-start.6 = (f32[5,512]{1,0:T(8,128)S(1)}, f32[5,512]{1,0:T(8,128)}, u32[]{:S(2)}) copy-start(f32[5,512]{1,0:T(8,128)} %blend_ref.1) | copy-start | bytes 30724
  12.5 0.7 %copy-start.7 = (f32[512]{0:T(512)S(1)}, f32[512]{0:T(512)}, u32[]{:S(2)}) copy-start(f32[512]{0:T(512)} %param.27) | copy-start | bytes 6148
  13.1 0.7 %copy-start.8 = (f32[512]{0:T(512)S(1)}, f32[512]{0:T(512)}, u32[]{:S(2)}) copy-start(f32[512]{0:T(512)} %param.30) | copy-start | bytes 6148
  13.8 0.7 %copy-start.9 = (f32[512]{0:T(512)S(1)}, f32[512]{0:T(512)}, u32[]{:S(2)}) copy-start(f32[512]{0:T(512)} %param.31) | copy-start | bytes 6148
  14.5 0.7 %copy-start.10 = (f32[512]{0:T(512)S(1)}, f32[512]{0:T(512)}, u32[]{:S(2)}) copy-start(f32[512]{0:T(512)} %param.32) | copy-start | bytes 6148
  15.2 0.7 %copy-start.11 = (s32[32]{0:T(128)S(1)}, s32[32]{0:T(128)}, u32[]{:S(2)}) copy-start(s32[32]{0:T(128)} %valid_ref.1) | copy-start | bytes 388
  15.8 0.7 %copy-start.12 = (s32[32]{0:T(128)S(1)}, s32[32]{0:T(128)}, u32[]{:S(2)}) copy-start(s32[32]{0:T(128)} %slot_ref.1) | copy-start | bytes 388

commit v2 on v1

--- a/solution.py
+++ b/solution.py
@@ -18,6 +18,10 @@
     return jnp.dot(a, b, preferred_element_type=F32)
 
 
+def dot_t(a, b):
+    return lax.dot_general(a, b, (((1,), (1,)), ((), ())), preferred_element_type=F32)
+
+
 def dot_split(a, ones):
     high = a.astype(BF16)
     low = (a - high.astype(F32)).astype(BF16)
@@ -37,10 +41,11 @@
 
 def kernel(
     sizes,
-    valid_ref, slot_ref, inv_ref,
-    x_ref, pages_hbm, shift_ref, blend_ref, w_hbm, fn_ref, fw_ref, fo_ref,
-    cn_ref, cw_ref, co_ref, eg_ref, ac_ref, rc_ref, gg_ref, fp_hbm,
+    valid_hbm, slot_hbm, x_hbm, pages_hbm, shift_hbm, blend_hbm, w_hbm, fn_hbm, fw_hbm, fo_hbm,
+    cn_hbm, cw_hbm, co_hbm, eg_hbm, ac_hbm, rc_hbm, gg_hbm, fp_hbm,
     mixed_ref, state_out, shift_out,
+    valid_ref, slot_ref, blend_ref, fn_ref, fw_ref, fo_ref,
+    cn_ref, cw_ref, co_ref, eg_ref, ac_ref, rc8_ref, gg8_ref,
     w_ref, pages_ref, fp_ref,
     x_all, shift_all, pack_out, pack_in, xs_ref, sh_ref, n_ref,
     part_send, part_recv, v_send, v_recv, sum_send, sum_all,
@@ -56,7 +61,7 @@
     TOK = RD * TS
     BT = TOK // H
     ZT = TOK // Z
-    DL = fn_ref.shape[1]
+    DL = fn_ref.shape[0]
     me_r, me_h, me_z = lax.axis_index("req"), lax.axis_index("head"), lax.axis_index("row")
     pending = []
 
@@ -73,10 +78,17 @@
         pending.append(c)
         return c
 
+    here_r = pl.multiple_of(me_r * RD, RD)
     loads = [
-        pltpu.make_async_copy(pages_hbm, pages_ref, local_sem.at[0]),
-        pltpu.make_async_copy(w_hbm, w_ref, local_sem.at[1]),
-        pltpu.make_async_copy(fp_hbm, fp_ref, local_sem.at[2]),
+        pltpu.make_async_copy(src, dst, local_sem.at[i])
+        for i, (src, dst) in enumerate([
+            (slot_hbm, slot_ref), (valid_hbm, valid_ref), (pages_hbm, pages_ref),
+            (x_hbm, x_all.at[me_h]), (shift_hbm, shift_all.at[pl.ds(here_r, RD)]),
+            (blend_hbm, blend_ref), (fn_hbm, fn_ref), (cn_hbm, cn_ref), (w_hbm, w_ref),
+            (fw_hbm, fw_ref), (cw_hbm, cw_ref), (fo_hbm, fo_ref), (co_hbm, co_ref),
+            (eg_hbm, eg_ref), (ac_hbm, ac_ref), (rc_hbm, rc8_ref), (gg_hbm, gg8_ref),
+            (fp_hbm, fp_ref),
+        ])
     ]
     for c in loads:
         c.start()
@@ -87,12 +99,10 @@
             pl.semaphore_signal(barrier, inc=1, device_id={axis: peer(axis, d)}, device_id_type=MESH)
     pl.semaphore_wait(barrier, R + H + Z - 3)
 
-    xc = [send(x_ref, x_all.at[me_h], sx, rx, "head", d) for d in range(1, H)]
-    shc = [send(shift_ref, shift_all.at[pl.ds(me_r * RD, RD)], ssh, rsh, "req", d) for d in range(1, R)]
-    x_all[me_h] = x_ref[...]
-    shift_all[pl.ds(pl.multiple_of(me_r * RD, RD), RD), :] = shift_ref[...]
-
-    loads[0].wait()
+    xc = [send(x_hbm, x_all.at[me_h], sx, rx, "head", d) for d in range(1, H)]
+    shc = [send(shift_hbm, shift_all.at[pl.ds(here_r, RD)], ssh, rsh, "req", d) for d in range(1, R)]
+    for c in loads[:3]:
+        c.wait()
     for p in range(RD):
         page = pages_ref[p]
         half = page.shape[1] // 2
@@ -118,19 +128,29 @@
     live = n_ref[...] > (trow & 3)
     live1 = live[:, :1]
 
+    def find(q, found):
+        page = slot_ref[q] - here_r
+        return tuple(jnp.where(page == p, q, f) for p, f in enumerate(found))
+
+    inv = lax.fori_loop(0, slot_ref.shape[0], find, (jnp.int32(0),) * RD)
+
+    for c in loads[3:8]:
+        c.wait()
     for c in xc + shc:
         c.wait_recv()
-    current = x_all[...].reshape(TOK, x_all.shape[2]).astype(F32)
-    xs_ref[...] = current
+    per = x_all.shape[1]
+    for r in range(RD):
+        xs_ref[pl.ds(TS * r, TS), :] = x_all[r // per, r % per].astype(F32)
+    current = xs_ref[...]
     for r in range(RD):
         sh_ref[pl.ds(TS * r, 1), :] = shift_all[pl.ds(slot_ref[me_r * RD + r], 1), :]
     wide, _ = iota2(current.shape)
     before = jnp.where((wide & 3) == 0, sh_ref[...], pltpu.roll(current, 1, 0))
     towards = before - current
     mixed_in = [(current + towards * blend_ref[b : b + 1, :]).astype(BF16) for b in range(5)]
-    d_part = dot(mixed_in[1], fn_ref[...])
-    l_part = dot(mixed_in[4], cn_ref[...])
-    loads[1].wait()
+    d_part = dot_t(mixed_in[1], fn_ref[...])
+    l_part = dot_t(mixed_in[4], cn_ref[...])
+    loads[8].wait()
     r_part = dot(mixed_in[0], w_ref[0])
     k_part = dot(mixed_in[2], w_ref[1])
     fill = jnp.zeros((TOK, 128 - DL), F32)
@@ -157,6 +177,11 @@
     sum_send[...] = total.astype(BF16)
     smc = [send(sum_send, sum_all.at[me_z], ssm, rsm, "row", d) for d in range(1, Z)]
     sum_all[me_z] = sum_send[...]
+
+    for c in loads[9:17]:
+        c.wait()
+    rc_row = jnp.concatenate([rc8_ref[h : h + 1, :] for h in range(8)], axis=1)
+    gg_row = jnp.concatenate([gg8_ref[h : h + 1, :] for h in range(8)], axis=1)
 
     for c in pgc:
         c.wait_recv()
@@ -190,7 +215,7 @@
     key_dir = scaled * lax.rsqrt(squares + 1e-6)
     key_adj = key_vec * (1.0 + (learn - 1.0) * ac_ref[...])
     bonus = jnp.where(
-        live, dot((query * key_adj * rc_ref[...]).astype(BF16), head_to_feature) * values, 0.0
+        live, dot((query * key_adj * rc_row).astype(BF16), head_to_feature) * values, 0.0
     )
     lane = lax.broadcasted_iota(jnp.int32, (TOK, 128), 1)
     low_half = lane < 64
@@ -265,9 +290,9 @@
     both = jnp.broadcast_to(both[:, None, :], (TOK // 8, 8, 128)).reshape(TOK, 128)
     mean = dot_split(jnp.where(slot_here & is_mean, both, 0.0), block16)
     scale = dot_split(jnp.where(slot_here & jnp.logical_not(is_mean), both, 0.0), block16)
-    normed = ((reading - mean) * scale * gg_ref[...] + bonus).astype(BF16)
-
-    loads[2].wait()
+    normed = ((reading - mean) * scale * gg_row + bonus).astype(BF16)
+
+    loads[17].wait()
     for q in range(Z):
         block = dot(normed, fp_ref[:, 512 * q : 512 * (q + 1)]).astype(BF16)
         for b in range(H):
@@ -277,7 +302,7 @@
     for c in bkc + lac:
         c.wait_recv()
     for p in range(RD):
-        q = inv_ref[me_r * RD + p]
+        q = inv[p]
         here = q - me_r * RD
         mine = jnp.logical_and(here >= 0, here < RD)
         at = jnp.clip(here, 0, RD - 1)
@@ -297,7 +322,8 @@
     for d in range(1, Z):
         fc[d - 1].wait_recv()
         res = res + fin_recv[d - 1].astype(F32)
-    mixed_ref[...] = res.astype(BF16)
+    for i in range(mixed_ref.shape[0]):
+        mixed_ref[i] = res[TS * i : TS * (i + 1)].astype(BF16)
     for c in pending:
         c.wait_send()
 
@@ -308,21 +334,24 @@
     wide = shift.shape[1]
     TOK = RD * TS
     BT, ZT = TOK // H, TOK // Z
-    everyone = jnp.arange(slots.shape[0], dtype=jnp.int32)
-    inv = jnp.sum(jnp.where(slots[None, :] == everyone[:, None], everyone[None, :], 0), axis=1)
     feats = gg.shape[0] * gg.shape[1]
     cols = w.shape[2]
     sums = 2 * cols + 256
-    smem = pl.BlockSpec(memory_space=pltpu.SMEM)
     vm = pl.BlockSpec(memory_space=pltpu.VMEM)
-    hbm = pl.BlockSpec(memory_space=pl.ANY)
+    hbm = pl.BlockSpec(memory_space=pltpu.HBM)
     V = pltpu.VMEM
     sems = []
     for n in (H, R, R, Z, Z, Z, Z, H, Z, R, R):
         sems += [pltpu.SemaphoreType.DMA((max(n - 1, 1),))] * 2
+    fn, cn = fn.T, cn.T
+    vec = (1, cols)
     scratch = [
+        pltpu.SMEM(valid.shape, jnp.int32), pltpu.SMEM(slots.shape, jnp.int32),
+        V(blend.shape, F32), V(fn.shape, BF16), V(fw.shape, BF16), V(vec, F32),
+        V(cn.shape, BF16), V(cw.shape, BF16), V(vec, F32), V(vec, F32), V(vec, F32),
+        V(rc.shape, F32), V(gg.shape, F32),
         V(w.shape, BF16), V(pages.shape, F32), V((feats, fp.shape[2]), BF16),
-        V((H, BT, wide), BF16), V((R * RD, wide), F32),
+        V((H,) + x.shape, BF16), V((R * RD, wide), F32),
         V((RD, 2 * heads, flat // 2), BF16), V((R * RD, 2 * heads, flat // 2), BF16),
         V((TOK, wide), F32), V((TOK, wide), F32), V((TOK, 128), jnp.int32),
         V((Z, ZT, sums), BF16), V((Z - 1, ZT, sums), BF16),
@@ -336,27 +365,27 @@
         V((TOK // 8, 128), F32), V((Z - 1, TOK // 8, 128), F32),
         V((H, Z, BT, wide), BF16), V((H - 1, Z, BT, wide), BF16),
         V((Z, BT, wide), BF16), V((Z - 1, BT, wide), BF16),
-        pltpu.SemaphoreType.DMA((3,)),
+        pltpu.SemaphoreType.DMA((18,)),
     ] + sems
     mixed, new_state, new_shift = pl.pallas_call(
         functools.partial(kernel, (R, H, Z)),
         out_shape=(
-            jax.ShapeDtypeStruct((BT, wide), BF16),
+            jax.ShapeDtypeStruct(x.shape, BF16),
             jax.ShapeDtypeStruct(pages.shape, F32),
             jax.ShapeDtypeStruct(shift.shape, F32),
         ),
-        in_specs=[smem] * 3 + [vm, hbm, vm, vm, hbm] + [vm] * 10 + [hbm],
+        in_specs=[hbm] * 18,
         out_specs=(vm, vm, vm),
         scratch_shapes=scratch,
         compiler_params=pltpu.CompilerParams(
-            collective_id=0, has_side_effects=True, vmem_limit_bytes=50 * 1024 * 1024
+            collective_id=0, has_side_effects=True, vmem_limit_bytes=63 * 1024 * 1024
         ),
     )(
-        valid, slots, inv, x.reshape(BT, wide), pages, shift, blend, w, fn, fw,
+        valid, slots, x, pages, shift, blend, w, fn, fw,
         fo.reshape(1, -1), cn, cw, co.reshape(1, -1), eg.reshape(1, -1), ac.reshape(1, -1),
-        rc.reshape(1, -1), gg.reshape(1, -1), fp.reshape(feats, -1),
-    )
-    return mixed.reshape(x.shape), new_state, new_shift
+        rc, gg, fp.reshape(feats, -1),
+    )
+    return mixed, new_state, new_shift
 
 
 def solution(mesh):

time: 54.8 us -> 41.5 us (0.76)
  local copies, waits for them, and re-layouts: 17.1 us -> 4.59 us
  other arithmetic: 0.77 us -> 0 us
    unnamed x30 -> x3, local copies, waits for them, and re-layouts: 14.2 us -> 4.59 us
    reshape x4 -> x0, local copies, waits for them, and re-layouts: 2.88 us -> none  [the longest x1 0.77 us: per_device(): rc.reshape(1, -1)]
    reduce_sum x1 -> x0, other arithmetic: 0.77 us -> none  [per_device(): jnp.sum(jnp.where(slots[None, :] == everyone[:, None], everyone[None, :],...]
where the time goes in v2:
time: 41.5 us; the launch traced here: 41.2 us
  Pallas kernels  36 us (87%)
  local copies, waits for them, and re-layouts  4.59 us (11%)
  between operations  0.65 us (2%)
    pallas_call x1, Pallas kernels, per_device(): pl.pallas_call(functools.partial(kernel, (R, H, Z)), out_shape=(jax.Shape...  36 us
    unnamed x3, local copies, waits for them, and re-layouts  4.59 us

profile of v2, /device:TPU:0, one launch (start us, length us, event | category | flops | bytes accessed | tf_op | source)
XLA Modules:
  0.0 41.2 jit_solution(14647754025638036659)
XLA Ops:
  0.6 36.0 %shard_map.193 = (bf16[4,4,512]{2,1,0:T(4,128)(2,1)}, f32[16,8,1024]{2,1,0:T(8,128)}, f32[16,512]{1,0:T(8,128)}) custom-call(s32[32]{0:T(128)} %valid_hbm.1, s32[32]{0:T(128)} %slot_hbm.1, bf16[4,4,512]{2,1,0:T(4,128)(2,1)} %x_hbm.1, f32[16,8,1024]{2,1,0:T(8,128)} %pages_hbm.1, f32[16,512]{1,0:T(8,128)} %shift_hbm.1, f32[5,512]{1,0:T(8,128)} %blend_hbm.1, ...), custom_call_target="tpu_custom_call" | custom-call | tf_op jit(solution)/shard_map/pallas_call | solution.py:370
  36.6 1.3 %copy.24 = bf16[4,4,512]{2,1,0:T(4,128)(2,1)} copy(bf16[4,4,512]{2,1,0:T(4,128)(2,1)} %get-tuple-element.6) | data formatting | bytes 32768
  37.9 1.9 %copy.25 = f32[16,8,1024]{2,1,0:T(8,128)} copy(f32[16,8,1024]{2,1,0:T(8,128)} %get-tuple-element.7) | data formatting | bytes 1048576
  39.8 1.4 %copy.26 = f32[16,512]{1,0:T(8,128)} copy(f32[16,512]{1,0:T(8,128)} %get-tuple-element.8) | data formatting | bytes 65536

commit v3 on v2

--- a/solution.py
+++ b/solution.py
@@ -46,7 +46,7 @@
     mixed_ref, state_out, shift_out,
     valid_ref, slot_ref, blend_ref, fn_ref, fw_ref, fo_ref,
     cn_ref, cw_ref, co_ref, eg_ref, ac_ref, rc8_ref, gg8_ref,
-    w_ref, pages_ref, fp_ref,
+    w_ref, pages_ref, fp_ref, state_buf,
     x_all, shift_all, pack_out, pack_in, xs_ref, sh_ref, n_ref,
     part_send, part_recv, v_send, v_recv, sum_send, sum_all,
     r_d, kd_d, kl_d, ka_d, dec_d, s_ref, read_ref,
@@ -109,30 +109,11 @@
         pack_out[p] = jnp.concatenate([page[:, :half], page[:, half:]], axis=0).astype(BF16)
     pgc = [send(pack_out, pack_in.at[pl.ds(me_r * RD, RD)], spg, rpg, "req", d) for d in range(1, R)]
 
-    row, col = iota2((512, 512))
-    same_head = as_ones((row >> 6) == (col >> 6))
-    to_rows = as_ones(
-        (((row >> 4) & 3) == (col >> 7)) & ((row >> 6) == ((col >> 4) & 7)) & ((row & 15) == (col & 15))
-    )
-    row, col = iota2((512, 128))
-    head_to_feature = as_ones((row >> 6) == (col >> 4))
-    row, col = iota2((128, 128))
-    half_sum = as_ones((row >> 6) == (col >> 6))
-    parity_sum = as_ones((row >> 6) == (col & 1))
-    block16 = as_ones((row >> 4) == (col >> 4))
-    row, col = iota2((128, 1024))
-    spread = as_ones((row & 15) == (col >> 6))
     for r in range(RD):
         n_ref[pl.ds(TS * r, TS), :] = jnp.full((TS, 128), valid_ref[me_r * RD + r], jnp.int32)
     trow, _ = iota2((TOK, 128))
     live = n_ref[...] > (trow & 3)
     live1 = live[:, :1]
-
-    def find(q, found):
-        page = slot_ref[q] - here_r
-        return tuple(jnp.where(page == p, q, f) for p, f in enumerate(found))
-
-    inv = lax.fori_loop(0, slot_ref.shape[0], find, (jnp.int32(0),) * RD)
 
     for c in loads[3:8]:
         c.wait()
@@ -157,6 +138,10 @@
     part = jnp.concatenate([r_part, k_part, d_part, fill, l_part, fill], axis=1)
     part_send[...] = part.astype(BF16).reshape(part_send.shape)
     ptc = [send(part_send.at[peer("row", d)], part_recv.at[d - 1], spt, rpt, "row", d) for d in range(1, Z)]
+    row, col = iota2((512, 512))
+    to_rows = as_ones(
+        (((row >> 4) & 3) == (col >> 7)) & ((row >> 6) == ((col >> 4) & 7)) & ((row & 15) == (col & 15))
+    )
     v_part = dot(dot(mixed_in[3], w_ref[2]).astype(BF16), to_rows)
     for q in range(Z):
         v_send[q] = v_part[:, 128 * q : 128 * (q + 1)].astype(BF16)
@@ -169,6 +154,22 @@
         send(last_all.at[pl.ds(base, RD)], last_all.at[pl.ds(base, RD)], sla, rla, "req", d)
         for d in range(1, R)
     ]
+
+    row, col = iota2((512, 512))
+    same_head = as_ones((row >> 6) == (col >> 6))
+    row, col = iota2((512, 128))
+    head_to_feature = as_ones((row >> 6) == (col >> 4))
+    row, col = iota2((128, 128))
+    half_sum = as_ones((row >> 6) == (col >> 6))
+    parity_sum = as_ones((row >> 6) == (col & 1))
+    block16 = as_ones((row >> 4) == (col >> 4))
+    row, col = iota2((128, 1024))
+    spread = as_ones((row & 15) == (col >> 6))
+    def find(q, found):
+        page = slot_ref[q] - here_r
+        return tuple(jnp.where(page == p, q, f) for p, f in enumerate(found))
+
+    inv = lax.fori_loop(0, slot_ref.shape[0], find, (jnp.int32(0),) * RD)
 
     total = part_send[me_z].astype(F32)
     for d in range(1, Z):
@@ -299,6 +300,12 @@
             out_send[b, q] = block[BT * b : BT * (b + 1)]
     oc = [send(out_send.at[peer("head", d)], out_recv.at[d - 1], so, ro, "head", d) for d in range(1, H)]
 
+    acc = out_send[me_h].astype(F32)
+    for d in range(1, H):
+        oc[d - 1].wait_recv()
+        acc = acc + out_recv[d - 1].astype(F32)
+    fin_send[...] = acc.astype(BF16)
+    fc = [send(fin_send.at[peer("row", d)], fin_recv.at[d - 1], sf, rf, "row", d) for d in range(1, Z)]
     for c in bkc + lac:
         c.wait_recv()
     for p in range(RD):
@@ -309,23 +316,32 @@
         got = back_in[q].astype(F32)
         for j in range(8):
             away = got[8 * (j >> 2) : 8 * (j >> 2) + 8, 128 * (j & 3) : 128 * (j & 3) + 128]
-            state_out[p, :, 128 * j : 128 * j + 128] = jnp.where(mine, s_ref[j, at], away)
+            state_buf[p, :, 128 * j : 128 * j + 128] = jnp.where(mine, s_ref[j, at], away)
         shift_out[pl.ds(p, 1), :] = last_all[pl.ds(q, 1), :]
 
-    acc = out_send[me_h].astype(F32)
-    for d in range(1, H):
-        oc[d - 1].wait_recv()
-        acc = acc + out_recv[d - 1].astype(F32)
-    fin_send[...] = acc.astype(BF16)
-    fc = [send(fin_send.at[peer("row", d)], fin_recv.at[d - 1], sf, rf, "row", d) for d in range(1, Z)]
+    stored = pltpu.make_async_copy(state_buf, state_out, local_sem.at[18])
+    stored.start()
+
     res = fin_send[me_z].astype(F32)
     for d in range(1, Z):
         fc[d - 1].wait_recv()
         res = res + fin_recv[d - 1].astype(F32)
     for i in range(mixed_ref.shape[0]):
         mixed_ref[i] = res[TS * i : TS * (i + 1)].astype(BF16)
+    stored.wait()
     for c in pending:
         c.wait_send()
+
+
+def hand_on(a, b, c, a_out, b_out, c_out, sem):
+    copies = [
+        pltpu.make_async_copy(src, dst, sem.at[i])
+        for i, (src, dst) in enumerate([(b, b_out), (a, a_out), (c, c_out)])
+    ]
+    for copy in copies:
+        copy.start()
+    for copy in copies:
+        copy.wait()
 
 
 def per_device(x, valid, slots, pages, shift, blend, w, fn, fw, fo, cn, cw, co, eg, ac, rc, gg, fp):
@@ -351,6 +367,7 @@
         V(cn.shape, BF16), V(cw.shape, BF16), V(vec, F32), V(vec, F32), V(vec, F32),
         V(rc.shape, F32), V(gg.shape, F32),
         V(w.shape, BF16), V(pages.shape, F32), V((feats, fp.shape[2]), BF16),
+        V(pages.shape, F32),
         V((H,) + x.shape, BF16), V((R * RD, wide), F32),
         V((RD, 2 * heads, flat // 2), BF16), V((R * RD, 2 * heads, flat // 2), BF16),
         V((TOK, wide), F32), V((TOK, wide), F32), V((TOK, 128), jnp.int32),
@@ -365,9 +382,9 @@
         V((TOK // 8, 128), F32), V((Z - 1, TOK // 8, 128), F32),
         V((H, Z, BT, wide), BF16), V((H - 1, Z, BT, wide), BF16),
         V((Z, BT, wide), BF16), V((Z - 1, BT, wide), BF16),
-        pltpu.SemaphoreType.DMA((18,)),
+        pltpu.SemaphoreType.DMA((19,)),
     ] + sems
-    mixed, new_state, new_shift = pl.pallas_call(
+    results = pl.pallas_call(
         functools.partial(kernel, (R, H, Z)),
         out_shape=(
             jax.ShapeDtypeStruct(x.shape, BF16),
@@ -375,7 +392,7 @@
             jax.ShapeDtypeStruct(shift.shape, F32),
         ),
         in_specs=[hbm] * 18,
-        out_specs=(vm, vm, vm),
+        out_specs=(vm, hbm, vm),
         scratch_shapes=scratch,
         compiler_params=pltpu.CompilerParams(
             collective_id=0, has_side_effects=True, vmem_limit_bytes=63 * 1024 * 1024
@@ -385,7 +402,14 @@
         fo.reshape(1, -1), cn, cw, co.reshape(1, -1), eg.reshape(1, -1), ac.reshape(1, -1),
         rc, gg, fp.reshape(feats, -1),
     )
-    return mixed, new_state, new_shift
+    return pl.pallas_call(
+        hand_on,
+        out_shape=tuple(jax.ShapeDtypeStruct(a.shape, a.dtype) for a in results),
+        in_specs=[hbm] * 3,
+        out_specs=(hbm,) * 3,
+        scratch_shapes=[pltpu.SemaphoreType.DMA((3,))],
+        compiler_params=pltpu.CompilerParams(vmem_limit_bytes=63 * 1024 * 1024),
+    )(*results)
 
 
 def solution(mesh):

time: 41.5 us -> 53.4 us (1.29)
  Pallas kernels: 36 us -> 52.6 us
  local copies, waits for them, and re-layouts: 4.59 us -> 0 us
    pallas_call x0 -> x1, Pallas kernels: none -> 18.5 us  [per_device(): pl.pallas_call(hand_on, out_shape=tuple((jax.ShapeDtypeStruct(a.shape, a....]
    unnamed x3 -> x0, local copies, waits for them, and re-layouts: 4.59 us -> none
    pallas_call x1, Pallas kernels: 36 us -> 34.1 us  [per_device(): pl.pallas_call(functools.partial(kernel, (R, H, Z)), out_shape=(jax.Shape...]
where the time goes in v3:
time: 53.4 us; the launch traced here: 53.2 us
  Pallas kernels  52.6 us (99%)
  between operations  0.65 us (1%)
    pallas_call x1, Pallas kernels, per_device(): pl.pallas_call(functools.partial(kernel, (R, H, Z)), out_shape=(jax.Shape...  34.1 us
    pallas_call x1, Pallas kernels, per_device(): pl.pallas_call(hand_on, out_shape=tuple((jax.ShapeDtypeStruct(a.shape, a....  18.5 us

profile of v3, /device:TPU:0, one launch (start us, length us, event | category | flops | bytes accessed | tf_op | source)
XLA Modules:
  0.0 53.2 jit_solution(16077569797980714506)
XLA Ops:
  0.6 34.1 %shard_map.193 = (bf16[4,4,512]{2,1,0:T(4,128)(2,1)}, f32[16,8,1024]{2,1,0:T(8,128)}, f32[16,512]{1,0:T(8,128)}) custom-call(s32[32]{0:T(128)} %valid_hbm.1, s32[32]{0:T(128)} %slot_hbm.1, bf16[4,4,512]{2,1,0:T(4,128)(2,1)} %x_hbm.1, f32[16,8,1024]{2,1,0:T(8,128)} %pages_hbm.1, f32[16,512]{1,0:T(8,128)} %shift_hbm.1, f32[5,512]{1,0:T(8,128)} %blend_hbm.1, ...), custom_call_target="tpu_custom_call" | custom-call | tf_op jit(solution)/shard_map/pallas_call | solution.py:387
  34.7 18.5 %shard_map.194 = (bf16[4,4,512]{2,1,0:T(4,128)(2,1)}, f32[16,8,1024]{2,1,0:T(8,128)}, f32[16,512]{1,0:T(8,128)}) custom-call(bf16[4,4,512]{2,1,0:T(4,128)(2,1)} %get-tuple-element.6.a, f32[16,8,1024]{2,1,0:T(8,128)} %get-tuple-element.7.b, f32[16,512]{1,0:T(8,128)} %get-tuple-element.8.c), custom_call_target="tpu_custom_call" | custom-call | tf_op jit(solution)/shard_map/pallas_call | solution.py:405

commit v4 on v3

--- a/solution.py
+++ b/solution.py
@@ -333,14 +333,16 @@
         c.wait_send()
 
 
-def hand_on(a, b, c, a_out, b_out, c_out, sem):
-    copies = [
-        pltpu.make_async_copy(src, dst, sem.at[i])
-        for i, (src, dst) in enumerate([(b, b_out), (a, a_out), (c, c_out)])
-    ]
-    for copy in copies:
+def hand_on(a, b, c, a_out, b_out, c_out, a_mid, b_mid, c_mid, sem_in, sem_out):
+    order = [(b, b_mid, b_out), (a, a_mid, a_out), (c, c_mid, c_out)]
+    into = [pltpu.make_async_copy(s, m, sem_in.at[i]) for i, (s, m, _) in enumerate(order)]
+    out = [pltpu.make_async_copy(m, o, sem_out.at[i]) for i, (_, m, o) in enumerate(order)]
+    for copy in into:
         copy.start()
-    for copy in copies:
+    for first, then in zip(into, out):
+        first.wait()
+        then.start()
+    for copy in out:
         copy.wait()
 
 
@@ -407,7 +409,7 @@
         out_shape=tuple(jax.ShapeDtypeStruct(a.shape, a.dtype) for a in results),
         in_specs=[hbm] * 3,
         out_specs=(hbm,) * 3,
-        scratch_shapes=[pltpu.SemaphoreType.DMA((3,))],
+        scratch_shapes=[V(a.shape, a.dtype) for a in results] + [pltpu.SemaphoreType.DMA((3,))] * 2,
         compiler_params=pltpu.CompilerParams(vmem_limit_bytes=63 * 1024 * 1024),
     )(*results)
 

time: 53.4 us -> 36.8 us (0.69)
  Pallas kernels: 52.6 us -> 36 us
    pallas_call x1, Pallas kernels: 18.5 us -> 1.89 us  [per_device(): pl.pallas_call(hand_on, out_shape=tuple((jax.ShapeDtypeStruct(a.shape, a....]
where the time goes in v4:
time: 36.8 us; the launch traced here: 36.6 us
  Pallas kernels  36 us (98%)
  between operations  0.65 us (2%)
    pallas_call x1, Pallas kernels, per_device(): pl.pallas_call(functools.partial(kernel, (R, H, Z)), out_shape=(jax.Shape...  34.1 us
    pallas_call x1, Pallas kernels, per_device(): pl.pallas_call(hand_on, out_shape=tuple((jax.ShapeDtypeStruct(a.shape, a....  1.89 us

profile of v4, /device:TPU:0, one launch (start us, length us, event | category | flops | bytes accessed | tf_op | source)
XLA Modules:
  0.0 36.6 jit_solution(8259124717793379571)
XLA Ops:
  0.6 34.1 %shard_map.193 = (bf16[4,4,512]{2,1,0:T(4,128)(2,1)}, f32[16,8,1024]{2,1,0:T(8,128)}, f32[16,512]{1,0:T(8,128)}) custom-call(s32[32]{0:T(128)} %valid_hbm.1, s32[32]{0:T(128)} %slot_hbm.1, bf16[4,4,512]{2,1,0:T(4,128)(2,1)} %x_hbm.1, f32[16,8,1024]{2,1,0:T(8,128)} %pages_hbm.1, f32[16,512]{1,0:T(8,128)} %shift_hbm.1, f32[5,512]{1,0:T(8,128)} %blend_hbm.1, ...), custom_call_target="tpu_custom_call" | custom-call | tf_op jit(solution)/shard_map/pallas_call | solution.py:389
  34.7 1.9 %shard_map.194 = (bf16[4,4,512]{2,1,0:T(4,128)(2,1)}, f32[16,8,1024]{2,1,0:T(8,128)}, f32[16,512]{1,0:T(8,128)}) custom-call(bf16[4,4,512]{2,1,0:T(4,128)(2,1)} %get-tuple-element.6.a, f32[16,8,1024]{2,1,0:T(8,128)} %get-tuple-element.7.b, f32[16,512]{1,0:T(8,128)} %get-tuple-element.8.c), custom_call_target="tpu_custom_call" | custom-call | tf_op jit(solution)/shard_map/pallas_call | solution.py:407
